TPU v7x, 256 devices: a whole 4x4x8 slice. The times are simulated.
256 devices in a mesh: rad: 4 (over y_hi, core), ang: 64 (over y_lo, z, x).
Axes of the slice: x: 4, y: 4 (y_hi: 2, y_lo: 2; y = y_hi * 2 + y_lo), z: 8, core: 2. Of those that a mesh axis runs over, the one named last changes fastest.
Arguments:
- adjoint_in: float32 [2, 2, 256, 256, 256], P(None, None, 'ang', 'rad'), may hold values from -6 to 6
- drift: float32 [256, 384, 768], P('rad', 'ang'), may hold values from -0.06 to 0.06
- induce: float32 [256, 384, 768], P('rad', 'ang'), may hold values from -6 to 6
- couple: float32 [256, 384, 768], P('rad', 'ang'), may hold values from -6 to 6
Outputs:
- adjoint_out: float32 [2, 2, 256, 256, 256], P(None, None, 'ang', 'rad')
All inputs are finite; a program needn't handle non-finite values.
Results may differ from a plain program's by a relative error of at most 0.0003.
Values sent between devices are 32-bit elements; how exact they have to be, the bound alone decides.
A program may use at most 64 MiB of HBM per device.

v0:
```python
import jax
import jax.numpy as jnp
from jax import lax
from jax.sharding import PartitionSpec as P

LMAX = 256
NLAT = 384
NLON = 768
RADII = 256


INNER = 7.0 / 13.0
DIFFUSE = 0.5


def radial_bands():
    index = jnp.arange(RADII, dtype=jnp.float32)
    radius = INNER + 0.5 * (1.0 - jnp.cos(jnp.pi * (index + 0.5) / RADII))
    gaps = radius[1:] - radius[:-1]
    below = jnp.concatenate([gaps[:1], gaps])
    above = jnp.concatenate([gaps, gaps[-1:]])
    lower = DIFFUSE * 2.0 / ((below + above) * below)
    upper = DIFFUSE * 2.0 / ((below + above) * above)
    degree = jnp.arange(LMAX, dtype=jnp.float32)
    horizontal = DIFFUSE * degree[:, None] * (degree[:, None] + 1.0) / (radius * radius)[None, :]
    middle = 1.0 + horizontal + lower[None, :] + upper[None, :]
    zero_one = jnp.zeros((1,), jnp.float32)
    sub_band = jnp.concatenate([zero_one, -upper[:-1]])
    super_band = jnp.concatenate([-lower[1:], zero_one])
    sub_band = jnp.broadcast_to(sub_band[None, :], middle.shape)
    super_band = jnp.broadcast_to(super_band[None, :], middle.shape)
    return (sub_band, middle, super_band)


def keep_mask(orders):
    degree = jnp.arange(LMAX, dtype=jnp.int32)
    keep_degree = degree[None, :] >= orders[:, None]
    sine_ok = jnp.stack([orders >= 0, orders != 0])
    return keep_degree[None, :, None, :] & sine_ok[:, :, None, None]


def latitude_weights():
    rows = jnp.arange(NLAT, dtype=jnp.float32)
    theta = jnp.pi * (rows + 0.5) / NLAT
    return jnp.pi / NLAT * jnp.sin(theta) * 0.5


def legendre_table(orders):
    rows = jnp.arange(NLAT, dtype=jnp.float32)
    theta = jnp.pi * (rows + 0.5) / NLAT
    cosine = jnp.cos(theta)
    sine = jnp.sin(theta)
    order_f = orders.astype(jnp.float32)
    half = jnp.full_like(order_f, 0.5)
    log_start = 0.5 * jnp.log(2.0 * order_f + 1.0) + 0.5 * (
        lax.lgamma(order_f + 0.5) - lax.lgamma(order_f + 1.0) - lax.lgamma(half)
    )
    start = jnp.exp(log_start[:, None] + order_f[:, None] * jnp.log(sine)[None, :])

    def advance(carry, degree):
        previous, earlier = carry
        deg_f = degree.astype(jnp.float32)
        above = degree > orders
        spread = jnp.where(above, deg_f * deg_f - order_f * order_f, 1.0)
        rise = jnp.sqrt(jnp.where(above, (4.0 * deg_f * deg_f - 1.0) / spread, 0.0))
        lower_deg = deg_f - 1.0
        damp = jnp.sqrt(
            jnp.maximum(
                (lower_deg * lower_deg - order_f * order_f) / (4.0 * lower_deg * lower_deg - 1.0),
                0.0,
            )
        )
        recur = rise[:, None] * (cosine[None, :] * previous - damp[:, None] * earlier)
        value = jnp.where(above[:, None], recur, jnp.where((degree == orders)[:, None], start, 0.0))
        return ((value, previous), value)

    zeros = jnp.zeros((orders.shape[0], NLAT), jnp.float32)
    unused, table = lax.scan(advance, (zeros, zeros), jnp.arange(LMAX, dtype=jnp.int32), unroll=16)
    return table


def trig_table():
    orders = jnp.arange(LMAX, dtype=jnp.int32)
    points = jnp.arange(NLON, dtype=jnp.int32)
    phase = orders[:, None] * points[None, :] % NLON
    angle = 2.0 * jnp.pi / NLON * phase.astype(jnp.float32)
    return jnp.stack([jnp.cos(angle), jnp.sin(angle)], axis=1)


def order_weights():
    orders = jnp.arange(LMAX, dtype=jnp.int32)
    return jnp.where(orders == 0, 1.0, 2.0).astype(jnp.float32) / NLON


def combine(harmonics, orders):
    order_f = orders.astype(jnp.float32)[:, None, None, None]
    plain = harmonics[0]
    shifted = harmonics[1]
    cos_part = plain[:, :, 0] - order_f * shifted[:, :, 1]
    sin_part = plain[:, :, 1] + order_f * shifted[:, :, 0]
    return jnp.stack([cos_part, sin_part], axis=3)


def shift_down(values, stride, fill):
    padding = jnp.full(values.shape[:1] + (stride,) + values.shape[2:], fill, values.dtype)
    return jnp.concatenate([padding, values[:, :-stride]], axis=1)


def shift_up(values, stride, fill):
    padding = jnp.full(values.shape[:1] + (stride,) + values.shape[2:], fill, values.dtype)
    return jnp.concatenate([values[:, stride:], padding], axis=1)


def cyclic_solve(sub_band, middle, super_band, rhs):
    rows = middle.shape[1]
    stride = 1
    while stride < rows:
        alpha = -sub_band / shift_down(middle, stride, 1.0)
        gamma = -super_band / shift_up(middle, stride, 1.0)
        new_middle = (
            middle
            + alpha * shift_down(super_band, stride, 0.0)
            + gamma * shift_up(sub_band, stride, 0.0)
        )
        rhs = (
            rhs
            + alpha[:, :, None] * shift_down(rhs, stride, 0.0)
            + gamma[:, :, None] * shift_up(rhs, stride, 0.0)
        )
        sub_band = alpha * shift_down(sub_band, stride, 0.0)
        super_band = gamma * shift_up(super_band, stride, 0.0)
        middle = new_middle
        stride = stride * 2
    return rhs / middle[:, :, None]


def solve_columns(sub_band, middle, super_band, masked):
    stacked = masked.transpose(4, 3, 0, 1, 2)
    solved = cyclic_solve(
        sub_band, middle, super_band, stacked.reshape(stacked.shape[0], stacked.shape[1], -1)
    )
    return solved.reshape(stacked.shape).transpose(2, 3, 4, 1, 0)


def regroup_solve(masked, sub_band, middle, super_band):
    solved = solve_columns(
        sub_band,
        middle,
        super_band,
        lax.all_to_all(masked, "rad", split_axis=2, concat_axis=3, tiled=True),
    )
    return lax.all_to_all(solved, "rad", split_axis=3, concat_axis=2, tiled=True)


def per_device(adjoint_in, drift, induce, couple):
    highest = lax.Precision.HIGHEST
    order_count = adjoint_in.shape[2]
    radius_count = adjoint_in.shape[3]
    lat_count = drift.shape[1]
    orders = lax.axis_index("ang") * order_count + jnp.arange(order_count, dtype=jnp.int32)
    masked = jnp.where(keep_mask(orders)[None], adjoint_in, 0.0)
    sub_band, middle, super_band = radial_bands()
    relaxed = regroup_solve(masked, sub_band, middle, super_band)
    table = legendre_table(orders)
    weights = latitude_weights()
    fourier = jnp.einsum("lmj,fcmrl->mjfcr", table, relaxed, precision=highest)
    fourier = (fourier * weights[None, :, None, None, None]).reshape(
        order_count, NLAT, 4 * radius_count
    )
    by_latitude = lax.all_to_all(fourier, "ang", split_axis=1, concat_axis=0, tiled=True)
    by_latitude = by_latitude.reshape(LMAX, lat_count, 2, 2, radius_count)
    trig = trig_table()
    weighted_trig = trig * order_weights()[:, None, None]
    grid_adjoint = jnp.einsum("mjfcr,mck->frjk", by_latitude, weighted_trig, precision=highest)
    plain = jnp.stack([couple * grid_adjoint[1], induce * grid_adjoint[0]])
    shifted = jnp.stack([-drift * grid_adjoint[0], -drift * grid_adjoint[1]])
    sources = jnp.stack([plain, shifted])
    harmonics = jnp.einsum("mck,sfrjk->smjcfr", trig, sources, precision=highest)
    combined = combine(harmonics, jnp.arange(LMAX, dtype=jnp.int32)).reshape(
        LMAX, lat_count, 4 * radius_count
    )
    by_order = lax.all_to_all(combined, "ang", split_axis=0, concat_axis=1, tiled=True)
    by_order = by_order.reshape(order_count, NLAT, 2, 2, radius_count)
    returned = jnp.einsum("lmj,mjfcr->fcmrl", table, by_order, precision=highest)
    return returned + relaxed


def solution(mesh):
    return jax.shard_map(
        per_device,
        mesh=mesh,
        in_specs=(
            P(None, None, "ang", "rad", None),
            P("rad", "ang", None),
            P("rad", "ang", None),
            P("rad", "ang", None),
        ),
        out_specs=P(None, None, "ang", "rad", None),
        check_vma=False,
    )
```

profile of v0, /device:TPU:6, one launch (start us, length us, event | category | flops | bytes accessed | tf_op | source)
XLA Modules:
  0.0 728.8 jit_solution(9180808748555208316)
XLA Ops:
  0.3 2.3 copy_select_fusion
  2.6 4.5 all-to-all-start
  7.9 1.4 fusion.135
  21.7 1.9 multiply_add_fusion.7
  33.8 1.8 copy.108
  35.6 4.8 all-to-all-start.1
  40.4 525.7 %while.21 = (s32[]{:T(128)}, f32[4,384]{1,0:T(4,128)S(1)}, f32[4,384]{1,0:T(4,128)S(1)}, f32[16,16,4,384]{3,2,1,0:T(4,128)S(1)}, s32[16,16]{1,0:T(8,128)S(1)}, /...) while((s32[]{:T(128)}, f32[4,384]{1,0:T(4,128)S(1)}, ...), condition=%wide.region_1.2_spmd.clone.clone.clone.clone, body=%wide.region_0.1_spmd.clone.clone.clone.clone.sunk | while | flops 202978 | bytes 705400 | solution.py:78
  42.5 1.4 fusion.235
  43.9 1.4 fusion.234
  75.3 1.4 fusion.235
  76.7 1.4 fusion.234
  108.2 1.4 fusion.235
  109.6 1.4 fusion.234
  141.0 1.4 fusion.235
  142.4 1.4 fusion.234
  173.9 1.4 fusion.235
  175.3 1.4 fusion.234
  206.7 1.4 fusion.235
  208.1 1.4 fusion.234
  239.6 1.4 fusion.235
  241.0 1.4 fusion.234
  272.4 1.4 fusion.235
  273.9 1.4 fusion.234
  305.3 1.4 fusion.235
  306.7 1.4 fusion.234
  338.2 1.4 fusion.235
  339.6 1.4 fusion.234
  371.0 1.4 fusion.235
  403.9 1.4 fusion.235
  405.3 1.4 fusion.234
  436.7 1.4 fusion.235
  469.6 1.4 fusion.235
  502.4 1.4 fusion.235
  535.3 1.4 fusion.235
  566.3 2.0 convolution_multiply_fusion
  568.3 1.6 copy.51
  569.9 12.1 %all-to-all-start.2 = ((f32[4,384,256]{2,0,1:T(4,128)}), f32[4,384,256]{2,0,1:T(4,128)S(1)}, u32[]{:S(2)}, u32[]{:S(2)}) async-start(f32[4,384,256]{2,0,1:T(4,128)} %copy.51), calls=%async_computation.2 | async-start | bytes 3145728 | tf_op jit(solution)/shard_map/all_to_all | solution.py:170
  582.0 4.4 fusion.126
  586.5 36.4 %all-to-all-done.2 = f32[4,384,256]{2,0,1:T(4,128)S(1)} async-done(((f32[4,384,256]{2,0,1:T(4,128)}), f32[4,384,256]{2,0,1:T(4,128)S(1)}, u32[]{:S(2)}, u32[]{:S(2)}) %all-to-all-start.2) | async-done | bytes 1572896 | tf_op jit(solution)/shard_map/all_to_all | solution.py:170
  622.8 1.4 copy.52
  624.2 3.6 reshape.1172
  627.9 7.5 %fusion.98 = f32[2,64,6,768]{3,1,0,2:T(8,128)S(1)} fusion(f32[256,6,2,2,64]{4,3,2,0,1:T(2,128)S(1)} %reshape.1172, f32[256,1,768]{2,0,1:T(8,128)} %get-tuple-element.661, f32[256,1,768]{2,0,1:T(8,128)} %get-tuple-element.662, f32[256]{0:T(256)S(1)} %fusion.138), kind=kOutput, calls=%fused_computation.168 | convolution fusion | flops 3624665088 | bytes 5506048 | tf_op jit(solution)/shard_map/mjfcr,mck->frjk/dot_general | solution.py:174
  637.6 16.8 %fusion.97 = f32[2,256,6,2,2,64]{1,5,3,2,4,0:T(8,128)S(1)} fusion(f32[1,2,64,6,768]{4,2,3,1,0:T(8,128)S(1)} %maximum_bitcast_fusion.3, f32[1,2,64,6,768]{4,2,3,1,0:T(8,128)S(1)} %maximum_bitcast_fusion.2, f32[256,1,768]{2,0,1:T(8,128)S(1)} %copy-done.1, f32[256,1,768]{2,0,1:T(8,128)S(1)} %copy-done.2), kind=kOutput, calls=%fused_computation.167 | convolution fusion | flops 7249330176 | bytes 9437184 | tf_op jit(solution)/shard_map/mck,sfrjk->smjcfr/dot_general | solution.py:178
  656.3 2.1 copy.58
  658.4 56.4 %all_to_all.54 = f32[256,6,256]{2,1,0:T(8,128)S(1)} all-to-all(f32[256,6,256]{2,1,0:T(8,128)S(1)} %copy.58), channel_id=1, replica_groups=mesh['rad'=4,'ang'=64] {'ang'}, dimensions={0} | all-to-all | bytes 3145728 | tf_op jit(solution)/shard_map/all_to_all | solution.py:182
  714.9 1.9 copy.107
  716.7 3.6 reshape.1174
  720.3 7.2 fusion.111
  (844 shorter events, 350.5 us)
Async XLA Ops:
  2.6 21.0 %all-to-all-start = ((f32[2,2,4,64,256]{4,3,1,0,2:T(8,128)}), f32[2,2,4,64,256]{4,3,1,0,2:T(8,128)S(1)}, u32[]{:S(2)}, u32[]{:S(2)}) async-start(f32[2,2,4,64,256]{4,3,1,0,2:T(8,128)} %copy_select_fusion), calls=%async_computation | async-start | bytes 2097152 | tf_op jit(solution)/shard_map/all_to_all | solution.py:150
  10.2 0.7 copy-start.4
  10.9 0.7 copy-start.6
  11.0 0.7 copy-start.8
  11.9 0.7 copy-start.10
  11.9 0.7 copy-start.12
  12.8 0.7 copy-start.14
  12.8 0.7 copy-start.16
  13.7 0.7 copy-start.18
  13.7 0.7 copy-start.20
  14.6 0.7 copy-start.22
  14.6 2.0 copy-start.24
  20.3 1.3 copy-start.28
  23.6 1.0 copy-start.5
  24.9 1.0 copy-start.7
  24.9 1.0 copy-start.9
  26.1 1.0 copy-start.11
  26.2 1.0 copy-start.13
  27.4 1.0 copy-start.15
  27.4 1.0 copy-start.17
  28.7 1.0 copy-start.19
  28.7 1.0 copy-start.21
  30.0 1.0 copy-start.23
  30.0 1.0 copy-start.25
  31.2 1.0 copy-start.26
  31.2 1.0 copy-start.27
  32.5 1.0 copy-start.32
  32.5 1.0 copy-start.33
  32.5 1.1 copy-start.34
  35.6 530.5 %all-to-all-start.1 = ((f32[2,2,1,256,256]{4,1,0,2,3:T(2,128)}), f32[2,2,1,256,256]{4,1,0,2,3:T(2,128)S(1)}, u32[]{:S(2)}, u32[]{:S(2)}) async-start(f32[2,2,1,256,256]{4,1,0,2,3:T(2,128)} %bitcast.398), calls=%async_computation.1 | async-start | bytes 2097152 | tf_op jit(solution)/shard_map/all_to_all | solution.py:152
  566.0 2.3 copy-start.3
  566.3 2.0 copy-start
  569.9 52.9 %all-to-all-start.2 = ((f32[4,384,256]{2,0,1:T(4,128)}), f32[4,384,256]{2,0,1:T(4,128)S(1)}, u32[]{:S(2)}, u32[]{:S(2)}) async-start(f32[4,384,256]{2,0,1:T(4,128)} %copy.51), calls=%async_computation.2 | async-start | bytes 3145728 | tf_op jit(solution)/shard_map/all_to_all | solution.py:170
  627.8 7.5 %copy-start.29 = (f32[64,6,768]{2,0,1:T(8,128)S(1)}, f32[64,6,768]{2,0,1:T(8,128)}, u32[]{:S(2)}) copy-start(f32[64,6,768]{2,0,1:T(8,128)} %param.7) | copy-start | bytes 3538948
  627.8 7.5 %copy-start.30 = (f32[64,6,768]{2,0,1:T(8,128)S(1)}, f32[64,6,768]{2,0,1:T(8,128)}, u32[]{:S(2)}) copy-start(f32[64,6,768]{2,0,1:T(8,128)} %param.9) | copy-start | bytes 3538948
  627.8 7.5 %copy-start.31 = (f32[64,6,768]{2,0,1:T(8,128)S(1)}, f32[64,6,768]{2,0,1:T(8,128)}, u32[]{:S(2)}) copy-start(f32[64,6,768]{2,0,1:T(8,128)} %param.8) | copy-start | bytes 3538948
  636.2 1.1 copy-start.1
  636.2 1.4 copy-start.2
where the time goes:
time: 743 us; the launch traced here: 729 us
  other arithmetic  365 us (49%)
  loops' own time  167 us (22%)
  blocking collectives  56.4 us (8%)
  local copies, waits for them, and re-layouts  47.8 us (6%)
  waiting for transfers between devices  36.4 us (5%)
  matrix products  33.5 us (5%)
  starting transfers between devices  21.3 us (3%)
    another operation x1, loops' own time, legendre_table(): lax.scan(advance, (zeros, zeros), jnp.arange(LMAX, dtype=jnp.int32), unro...  167 us
    sqrt x128, other arithmetic, advance(): rise = jnp.sqrt(jnp.where(above, (4.0 * deg_f * deg_f - 1.0) / spread, 0.0))  161 us
    eq x128, other arithmetic, advance(): degree == orders  160 us
    all_to_all x1, blocking collectives, per_device(): lax.all_to_all(combined, 'ang', split_axis=0, concat_axis=1, tiled=True)  56.4 us
    all_to_all x1, waiting for transfers between devices, per_device(): lax.all_to_all(fourier, 'ang', split_axis=1, concat_axis=0, tiled=True)  36.4 us
    while x240, other arithmetic  20.8 us
    dot_general x1, matrix products, per_device(): jnp.einsum('mck,sfrjk->smjcfr', trig, sources, precision=highest)  16.8 us
  transfers between devices with their start and end apart: 3, of which 1 were waited for; matrix products, arithmetic and copies ran while one was open for 52% of the time, Pallas kernels for 0%

commit v1 on v0

v1 whole, which is shorter than its diff:
```python
import functools

import jax
import jax.numpy as jnp
import ml_dtypes
import numpy as np
from jax import lax
from jax.experimental import pallas as pl
from jax.experimental.pallas import tpu as pltpu
from jax.sharding import PartitionSpec as P

LMAX = 256
NLAT = 384
NLON = 768
RADII = 256
RAD = 4
ANG = 64
SHELLS = RADII // RAD
INNER = 7.0 / 13.0
DIFFUSE = 0.5
F32 = jnp.float32
BF16 = jnp.bfloat16
MESH = pl.DeviceIdType.MESH


def split_np(array):
    high = array.astype(np.float32).astype(ml_dtypes.bfloat16)
    low = (array - high.astype(np.float64)).astype(np.float32).astype(ml_dtypes.bfloat16)
    return high, low


@functools.cache
def radial_constants():
    index = np.arange(RADII, dtype=np.float64)
    radius = INNER + 0.5 * (1.0 - np.cos(np.pi * (index + 0.5) / RADII))
    gaps = np.diff(radius)
    below = np.concatenate([gaps[:1], gaps])
    above = np.concatenate([gaps, gaps[-1:]])
    lower = DIFFUSE * 2.0 / ((below + above) * below)
    upper = DIFFUSE * 2.0 / ((below + above) * above)
    degree = np.arange(LMAX, dtype=np.float64)
    middle = 1.0 + DIFFUSE * (degree * (degree + 1.0))[None, :] / (radius * radius)[:, None]
    middle = middle + (lower + upper)[:, None]
    sub = np.concatenate([[0.0], -upper[:-1]])
    sup = np.concatenate([-lower[1:], [0.0]])
    inverse = np.zeros((RAD, SHELLS, LMAX))
    forward = np.zeros((RAD, SHELLS, LMAX))
    backward = np.zeros((RAD, SHELLS, LMAX))
    after = np.zeros((RAD, SHELLS, LMAX))
    before = np.zeros((RAD, SHELLS, LMAX))
    for block in range(RAD):
        base = block * SHELLS
        ratio = np.zeros((LMAX,))
        for row in range(SHELLS):
            here = sub[base + row] if row else 0.0
            inverse[block, row] = 1.0 / (middle[base + row] - here * ratio)
            forward[block, row] = -here * inverse[block, row]
            ratio = sup[base + row] * inverse[block, row]
            backward[block, row] = -ratio if row < SHELLS - 1 else 0.0

        def local_solve(right):
            swept = np.zeros((SHELLS, LMAX))
            carry = np.zeros((LMAX,))
            for row in range(SHELLS):
                carry = right[row] * inverse[block, row] + forward[block, row] * carry
                swept[row] = carry
            carry = np.zeros((LMAX,))
            for row in range(SHELLS - 1, -1, -1):
                carry = swept[row] + backward[block, row] * carry
                swept[row] = carry
            return swept

        last = np.zeros((SHELLS, LMAX))
        last[-1] = -sup[base + SHELLS - 1]
        first = np.zeros((SHELLS, LMAX))
        first[0] = -sub[base]
        after[block] = local_solve(last)
        before[block] = local_solve(first)
    coupling = np.zeros((LMAX, 2 * RAD, 2 * RAD))
    for block in range(RAD):
        for end, row in ((0, 0), (1, SHELLS - 1)):
            if block < RAD - 1:
                coupling[:, 2 * block + end, 2 * (block + 1)] = after[block, row]
            if block:
                coupling[:, 2 * block + end, 2 * (block - 1) + 1] = before[block, row]
    reduced = np.linalg.inv(np.eye(2 * RAD)[None] - coupling)
    ends = np.zeros((RAD, 2, 2 * RAD, LMAX))
    for block in range(RAD):
        if block < RAD - 1:
            ends[block, 0] = reduced[:, 2 * (block + 1), :].T
        if block:
            ends[block, 1] = reduced[:, 2 * (block - 1) + 1, :].T
    packed = np.concatenate(
        [inverse, forward, backward, after, before, ends.reshape(RAD, 4 * RAD, LMAX)], axis=1
    )
    halves = packed.reshape(RAD, 5 * SHELLS + 4 * RAD, 2, 128).transpose(0, 2, 1, 3)
    return np.ascontiguousarray(halves.astype(np.float32))


def latitude_of():
    place = np.arange(12)[:, None]
    lane = np.arange(128)[None, :] % 32
    return 6 * ((place % 2) * 32 + lane) + place // 2


@functools.cache
def legendre_constants():
    with jax.ensure_compile_time_eval(), jax.default_device(jax.devices("cpu")[0]):
        order = jnp.arange(LMAX, dtype=F32)
        log_start = 0.5 * jnp.log(2.0 * order + 1.0) + 0.5 * (
            lax.lgamma(order + 0.5) - lax.lgamma(order + 1.0) - lax.lgamma(jnp.float32(0.5))
        )
        theta = jnp.pi * (jnp.arange(NLAT, dtype=F32) + 0.5) / NLAT
        sine = np.asarray(jnp.log(jnp.sin(theta)))
        cosine = np.asarray(jnp.cos(theta))
        log_start = np.asarray(log_start)
    exponent = log_start[:, None] + (np.arange(LMAX, dtype=np.float32)[:, None] * sine[None, :])
    start = np.exp(exponent.astype(np.float32).astype(np.float64)).astype(np.float32)
    start = np.where(start < np.float32(1.1754944e-38), np.float32(0.0), start)
    rows = latitude_of()
    orders = np.arange(128) // 32
    table = np.zeros((ANG, 16, 128), np.float32)
    for block in range(ANG):
        table[block, :12] = start[4 * block + orders[None, :], rows]
    angle = np.zeros((16, 128), np.float32)
    angle[:12] = cosine[rows]
    return table, angle


@functools.cache
def weight_constants():
    rows = 6 * np.arange(ANG)[:, None] + np.arange(6)[None, :]
    theta = np.pi * (rows + 0.5) / NLAT
    weights = np.zeros((ANG, 8, 128), np.float32)
    weights[:, :6, :] = (np.pi / NLAT * np.sin(theta) * 0.5)[:, :, None]
    return weights


@functools.cache
def trig_constants():
    order = np.arange(LMAX)
    point = np.arange(NLON)
    angle = 2.0 * np.pi / NLON * ((order[:, None] * point[None, :]) % NLON)
    cosine, sine = np.cos(angle), np.sin(angle)
    weight = np.where(order == 0, 1.0, 2.0)[:, None] / NLON
    onto_grid = np.stack([cosine * weight, sine * weight], axis=1).reshape(2 * LMAX, NLON).T
    plain = np.stack([cosine, sine], axis=1).reshape(2 * LMAX, NLON)
    shifted = np.stack([-sine * order[:, None], cosine * order[:, None]], axis=1)
    shifted = shifted.reshape(2 * LMAX, NLON)
    onto_grid = onto_grid.reshape(3, 256, 2 * LMAX)
    back = np.stack([plain.reshape(512, 3, 256), shifted.reshape(512, 3, 256)], axis=2)
    back = back.transpose(1, 0, 2, 3).reshape(3, 512, 512)
    return split_np(onto_grid) + split_np(back)


def split(value):
    high = value.astype(BF16)
    return high, (value - high.astype(F32)).astype(BF16)


NN = (((1,), (0,)), ((), ()))
NT = (((1,), (1,)), ((), ()))


def product(left, right, dims):
    dot = functools.partial(lax.dot_general, dimension_numbers=dims, preferred_element_type=F32)
    return dot(left[0], right[0]) + (dot(left[0], right[1]) + dot(left[1], right[0]))


def kernel(
    adj_hbm, drift_hbm, induce_hbm, couple_hbm, tri_hbm, start_hbm, weight_hbm, angle_ref,
    wh_hbm, wl_hbm, ah_hbm, al_hbm,
    out_ref,
    adj, rel, tri, start, weight, tb, rise_ref, damp_ref, tth, ttl, rbh, rbl,
    ends, xs, xr, cs, yr, drift, induce, couple, mp, md, wh, wl, ah, al, acc,
    in_sem, ends_send, ends_recv, xs_sem, xr_sem, cs_sem, yr_sem,
):
    rho = lax.axis_index("rad")
    me = lax.axis_index("ang")
    y, z, x = me // 32, lax.rem(me // 4, 8), lax.rem(me, 4)

    def peer(step):
        other = lax.rem(step * 37, 64)
        py = lax.rem(y + other // 32, 2)
        pz = lax.rem(z + lax.rem(other // 4, 8), 8)
        px = lax.rem(x + lax.rem(other, 4), 4)
        return py * 32 + pz * 4 + px

    def rad_peer(step):
        return lax.rem(rho + step, RAD)

    loads = [
        pltpu.make_async_copy(adj_hbm.at[:, pl.ds(0, 128)], adj.at[0], in_sem.at[0]),
        pltpu.make_async_copy(adj_hbm.at[:, pl.ds(128, 128)], adj.at[1], in_sem.at[1]),
        pltpu.make_async_copy(tri_hbm.at[rho], tri, in_sem.at[2]),
        pltpu.make_async_copy(start_hbm.at[me], start, in_sem.at[3]),
        pltpu.make_async_copy(weight_hbm.at[me], weight, in_sem.at[4]),
        pltpu.make_async_copy(wh_hbm, wh, in_sem.at[5]),
        pltpu.make_async_copy(wl_hbm, wl, in_sem.at[6]),
        pltpu.make_async_copy(ah_hbm, ah, in_sem.at[7]),
        pltpu.make_async_copy(al_hbm, al, in_sem.at[8]),
        pltpu.make_async_copy(drift_hbm, drift, in_sem.at[9]),
        pltpu.make_async_copy(induce_hbm, induce, in_sem.at[10]),
        pltpu.make_async_copy(couple_hbm, couple, in_sem.at[11]),
    ]
    for load in loads:
        load.start()

    barrier = pltpu.get_barrier_semaphore()

    def greet(step, unused):
        pl.semaphore_signal(barrier, inc=1, device_id=(rho, peer(step)), device_id_type=MESH)
        return unused

    for step in range(1, RAD):
        pl.semaphore_signal(barrier, inc=1, device_id=(rad_peer(step), me), device_id_type=MESH)
    lax.fori_loop(1, ANG, greet, 0)

    lane_order = 4 * me + lax.broadcasted_iota(jnp.int32, (32, 128), 1) // 32
    order_f = lane_order.astype(F32)

    def factors(block, unused):
        degree = block * 32 + lax.broadcasted_iota(jnp.int32, (32, 128), 0)
        deg_f = degree.astype(F32)
        above = degree > lane_order
        spread = jnp.where(above, deg_f * deg_f - order_f * order_f, 1.0)
        square = jnp.where(above, (4.0 * deg_f * deg_f - 1.0) / spread, 1.0)
        rise_ref[pl.ds(block * 32, 32), :] = jnp.where(above, jnp.sqrt(square), 0.0)
        low = deg_f - 1.0
        square = jnp.maximum((low * low - order_f * order_f) / (4.0 * low * low - 1.0), 0.0)
        damp_ref[pl.ds(block * 32, 32), :] = jnp.sqrt(square)
        return unused

    lax.fori_loop(0, 8, factors, 0)

    for load in loads[:3]:
        load.wait()
    row_id = lax.broadcasted_iota(jnp.int32, (16, 128), 0)
    row_order = 4 * me + lax.rem(row_id, 4)
    sine_zero = jnp.logical_and(row_order == 0, lax.rem(row_id // 4, 2) == 1)
    lanes = lax.broadcasted_iota(jnp.int32, (16, 128), 1)
    keeps = [
        jnp.logical_and(lanes + 128 * half >= row_order, jnp.logical_not(sine_zero))
        for half in range(2)
    ]

    def tri_row(row, half):
        return tri[half, pl.ds(row, 1), :]

    def sweep(row, carry):
        result = []
        for half in range(2):
            right = adj[half, pl.ds(row, 16, stride=64), :]
            right = jnp.where(keeps[half], right, 0.0) * tri_row(row, half)
            value = right + tri_row(SHELLS + row, half) * carry[half]
            rel[half, pl.ds(row, 16, stride=64), :] = value
            result.append(value)
        return tuple(result)

    zero = jnp.zeros((16, 128), F32)
    blank = jnp.where(keeps[0], 0.0, zero)
    lax.fori_loop(0, SHELLS, sweep, (blank, blank), unroll=4)

    def unsweep(step, carry):
        row = SHELLS - 1 - step
        result = []
        for half in range(2):
            value = rel[half, pl.ds(row, 16, stride=64), :]
            value = value + tri_row(2 * SHELLS + row, half) * carry[half]
            rel[half, pl.ds(row, 16, stride=64), :] = value
            result.append(value)
        return tuple(result)

    lax.fori_loop(0, SHELLS, unsweep, (blank, blank), unroll=4)
    for half in range(2):
        for end, row in ((0, 0), (1, SHELLS - 1)):
            ends[rho, pl.ds(16 * end, 16), 128 * half : 128 * half + 128] = rel[
                half, pl.ds(row, 16, stride=64), :
            ]

    pl.semaphore_wait(barrier, ANG - 1 + RAD - 1)
    for step in range(1, RAD):
        pltpu.make_async_remote_copy(
            src_ref=ends.at[rho],
            dst_ref=ends.at[rho],
            send_sem=ends_send,
            recv_sem=ends_recv,
            device_id=(rad_peer(step), me),
            device_id_type=MESH,
        ).start()

    loads[3].wait()
    cosine = angle_ref[...]
    begin = start[...]
    nothing = begin * 0.0
    wide_order = 4 * me + lax.broadcasted_iota(jnp.int32, (16, 128), 1) // 32

    def advance(degree, carry):
        previous, earlier = carry
        rise = rise_ref[pl.ds(degree, 1), :]
        damp = damp_ref[pl.ds(degree, 1), :]
        value = rise * (cosine * previous - damp * earlier)
        value = jnp.where(wide_order == degree, begin, value)
        tb[pl.ds(pl.multiple_of(degree * 16, 16), 16), :] = value
        return value, previous

    lax.fori_loop(0, LMAX, advance, (nothing, nothing), unroll=8)

    for place in range(12):
        turned = tb[pl.ds(place, LMAX, stride=16), :].T
        high, low = split(turned)
        for order in range(4):
            tth[order, 32 * place : 32 * place + 32, :] = high[32 * order : 32 * order + 32]
            ttl[order, 32 * place : 32 * place + 32, :] = low[32 * order : 32 * order + 32]

    block_ends = ends.at[pl.ds(0, RAD - 1)]
    pltpu.make_async_copy(block_ends, block_ends, ends_recv).wait()
    outer = []
    for half in range(2):
        cols = slice(128 * half, 128 * half + 128)
        pair = []
        for side in range(2):
            total = zero
            for source in range(RAD):
                for end in range(2):
                    factor = tri_row(5 * SHELLS + 8 * side + 2 * source + end, half)
                    total = total + factor * ends[source, 16 * end : 16 * end + 16, cols]
            pair.append(total)
        outer.append(pair)

    def correct(row, unused):
        for half in range(2):
            value = rel[half, pl.ds(row, 16, stride=64), :]
            value = value + tri_row(3 * SHELLS + row, half) * outer[half][0]
            value = value + tri_row(4 * SHELLS + row, half) * outer[half][1]
            rel[half, pl.ds(row, 16, stride=64), :] = value
        return unused

    lax.fori_loop(0, SHELLS, correct, 0, unroll=4)

    for order in range(4):
        for part in range(2):
            for field in range(2):
                rows = pl.ds(((2 * field + part) * 4 + order) * 64, 64)
                value = jnp.concatenate([rel[0, rows, :], rel[1, rows, :]], axis=1)
                high, low = split(value)
                at = (2 * part + field) * 64
                rbh[order, at : at + 64, :] = high
                rbl[order, at : at + 64, :] = low
                acc[order, at : at + 64, :] = value

    def send_part(part, source, target, send_sem, recv_sem):
        def send(step, unused):
            other = peer(step)
            pltpu.make_async_remote_copy(
                src_ref=source.at[pl.ds(2 * part, 2), pl.ds(pl.multiple_of(other * 8, 8), 8), :],
                dst_ref=target.at[pl.ds(2 * part, 2), pl.ds(pl.multiple_of(me * 8, 8), 8), :],
                send_sem=send_sem.at[part],
                recv_sem=recv_sem.at[part],
                device_id=(rho, other),
                device_id_type=MESH,
            ).start()
            return unused

        lax.fori_loop(1, ANG, send, 0)
        own = pl.ds(pl.multiple_of(me * 8, 8), 8)
        for t in range(2 * part, 2 * part + 2):
            target[t, own, :] = source[t, own, :]

    def wait_part(part, target, sem):
        block = target.at[pl.ds(2 * part, 2), pl.ds(0, (ANG - 1) * 8), :]
        pltpu.make_async_copy(block, block, sem.at[part]).wait()

    for part in range(3):
        rows = slice(128 * part, 128 * part + 128)
        for order in range(4):
            value = product(
                (tth[order, rows, :], ttl[order, rows, :]), (rbh[order], rbl[order]), NT
            )
            for trig in range(2):
                for t in range(2):
                    xs[2 * part + t, pl.ds(2 * order + trig, 64, stride=8), :] = value[
                        64 * t : 64 * t + 64, 128 * trig : 128 * trig + 128
                    ]
        send_part(part, xs, xr, xs_sem, xr_sem)

    for load in loads[4:]:
        load.wait()
    for t in range(6):
        for block in range(6):
            cols = slice(128 * block, 128 * block + 128)
            scale = weight[t : t + 1, :]
            pair = jnp.concatenate([couple[:, t, cols], induce[:, t, cols]], axis=0)
            mp[t, cols, :] = pair.T * scale
            turn = drift[:, t, cols]
            md[t, cols, :] = jnp.concatenate([turn, turn], axis=0).T * (-scale)

    for part in range(3):
        wait_part(part, xr, xr_sem)
        first, second = 2 * part, 2 * part + 1
        field = split(jnp.concatenate([xr[first], xr[second]], axis=1))

        acc_c = jnp.zeros((512, 256), F32)
        for block in range(3):
            grid = product((wh[block], wl[block]), field, NN)
            rows = slice(256 * block, 256 * block + 256)
            sides = []
            for t in range(2):
                here = grid[:, 128 * t : 128 * t + 128]
                plain = mp[2 * part + t, rows, :] * pltpu.roll(here, 64, 1)
                sides.append(jnp.concatenate([plain, md[2 * part + t, rows, :] * here], axis=0))
            source = split(jnp.concatenate(sides, axis=1))
            acc_c = acc_c + product((ah[block], al[block]), source, NN)
        cs[first] = acc_c[:, :128]
        cs[second] = acc_c[:, 128:]
        send_part(part, cs, yr, cs_sem, yr_sem)

    for part in range(3):
        wait_part(part, yr, yr_sem)
        rows = slice(128 * part, 128 * part + 128)
        for order in range(4):
            sides = []
            for trig in range(2):
                pair = [yr[2 * part + t, pl.ds(2 * order + trig, 64, stride=8), :] for t in range(2)]
                sides.append(jnp.concatenate(pair, axis=0).T)
            value = split(jnp.concatenate(sides, axis=0))
            acc[order] = acc[order] + product(value, (tth[order, rows, :], ttl[order, rows, :]), NN)

    for order in range(4):
        for trig in range(2):
            for field in range(2):
                at = ((2 * field + trig) * 4 + order) * 64
                here = (2 * trig + field) * 64
                out_ref[at : at + 64, :] = acc[order, here : here + 64, :]

    pltpu.make_async_copy(block_ends, block_ends, ends_send).wait()
    for part in range(3):
        wait_part(part, xs, xs_sem)
        wait_part(part, cs, cs_sem)


def per_device(adjoint_in, drift, induce, couple):
    wh, wl, ah, al = trig_constants()
    start, angle = legendre_constants()
    anywhere = pl.BlockSpec(memory_space=pl.ANY)
    vmem = pl.BlockSpec(memory_space=pltpu.VMEM)
    result = pl.pallas_call(
        kernel,
        out_shape=jax.ShapeDtypeStruct((1024, LMAX), F32),
        in_specs=[anywhere] * 7 + [vmem] + [anywhere] * 4,
        out_specs=vmem,
        scratch_shapes=[
            pltpu.VMEM((2, 1024, 128), F32),
            pltpu.VMEM((2, 1024, 128), F32),
            pltpu.VMEM((2, 336, 128), F32),
            pltpu.VMEM((16, 128), F32),
            pltpu.VMEM((8, 128), F32),
            pltpu.VMEM((LMAX * 16, 128), F32),
            pltpu.VMEM((LMAX, 128), F32),
            pltpu.VMEM((LMAX, 128), F32),
            pltpu.VMEM((4, NLAT, LMAX), BF16),
            pltpu.VMEM((4, NLAT, LMAX), BF16),
            pltpu.VMEM((4, 256, LMAX), BF16),
            pltpu.VMEM((4, 256, LMAX), BF16),
            pltpu.VMEM((RAD, 32, LMAX), F32),
            pltpu.VMEM((6, 512, 128), F32),
            pltpu.VMEM((6, 512, 128), F32),
            pltpu.VMEM((6, 512, 128), F32),
            pltpu.VMEM((6, 512, 128), F32),
            pltpu.VMEM((SHELLS, 6, NLON), F32),
            pltpu.VMEM((SHELLS, 6, NLON), F32),
            pltpu.VMEM((SHELLS, 6, NLON), F32),
            pltpu.VMEM((6, NLON, 128), F32),
            pltpu.VMEM((6, NLON, 128), F32),
            pltpu.VMEM((3, 256, 512), BF16),
            pltpu.VMEM((3, 256, 512), BF16),
            pltpu.VMEM((3, 512, 512), BF16),
            pltpu.VMEM((3, 512, 512), BF16),
            pltpu.VMEM((4, 256, LMAX), F32),
            pltpu.SemaphoreType.DMA((12,)),
            pltpu.SemaphoreType.DMA,
            pltpu.SemaphoreType.DMA,
            pltpu.SemaphoreType.DMA((3,)),
            pltpu.SemaphoreType.DMA((3,)),
            pltpu.SemaphoreType.DMA((3,)),
            pltpu.SemaphoreType.DMA((3,)),
        ],
        compiler_params=pltpu.CompilerParams(
            collective_id=0, has_side_effects=True, vmem_limit_bytes=56 * 1024 * 1024
        ),
    )(
        adjoint_in.reshape(1024, LMAX), drift, induce, couple,
        jnp.asarray(radial_constants()), jnp.asarray(start), jnp.asarray(weight_constants()),
        jnp.asarray(angle), jnp.asarray(wh), jnp.asarray(wl), jnp.asarray(ah), jnp.asarray(al),
    )
    return result.reshape(2, 2, 4, SHELLS, LMAX)


def solution(mesh):
    return jax.shard_map(
        per_device,
        mesh=mesh,
        in_specs=(
            P(None, None, "ang", "rad", None),
            P("rad", "ang", None),
            P("rad", "ang", None),
            P("rad", "ang", None),
        ),
        out_specs=P(None, None, "ang", "rad", None),
        check_vma=False,
    )
```

time: 743 us -> 102 us (0.14); the launches traced: 729 us -> 101 us
  other arithmetic: 365 us -> 0 us
  loops' own time: 167 us -> 0 us
  Pallas kernels: 0 us -> 91.6 us
  blocking collectives: 56.4 us -> 0 us
  local copies, waits for them, and re-layouts: 47.8 us -> 9.25 us
  waiting for transfers between devices: 36.4 us -> 0 us
  matrix products: 33.5 us -> 0 us
  starting transfers between devices: 21.3 us -> 0 us
    another operation x1 -> x0, loops' own time: 167 us -> none  [legendre_table(): lax.scan(advance, (zeros, zeros), jnp.arange(LMAX, dtype=jnp.int32), unro...]
    sqrt x256 -> x0, other arithmetic: 163 us -> none  [the longest x128 161 us: advance(): rise = jnp.sqrt(jnp.where(above, (4.0 * deg_f * deg_f - 1.0) / spread, 0.0))]
    eq x128 -> x0, other arithmetic: 160 us -> none  [advance(): degree == orders]
    pallas_call x0 -> x1, Pallas kernels: none -> 91.6 us  [per_device(): pl.pallas_call(kernel, out_shape=jax.ShapeDtypeStruct((1024, LMAX), F32),...]
    all_to_all x1 -> x0, blocking collectives: 56.4 us -> none  [per_device(): lax.all_to_all(combined, 'ang', split_axis=0, concat_axis=1, tiled=True)]
    all_to_all x3 -> x0, waiting for transfers between devices: 36.4 us -> none  [the longest x1 36.4 us: per_device(): lax.all_to_all(fourier, 'ang', split_axis=1, concat_axis=0, tiled=True)]
    dot_general x4 -> x0, matrix products: 33.5 us -> none  [the longest x1 16.8 us: per_device(): jnp.einsum('mck,sfrjk->smjcfr', trig, sources, precision=highest)]
    all_to_all x3 -> x0, starting transfers between devices: 21.3 us -> none  [the longest x1 12.1 us: per_device(): lax.all_to_all(fourier, 'ang', split_axis=1, concat_axis=0, tiled=True)]
  transfers between devices with their start and end apart: 3 -> 0, of which waited for: 1 -> 0; matrix products, arithmetic and copies ran while one was open for 52% -> 0% of each run, Pallas kernels for 0% -> 0%
where the time goes in v1:
time: 102 us; the launch traced here: 101 us
  Pallas kernels  91.6 us (90%)
  local copies, waits for them, and re-layouts  9.25 us (9%)
    pallas_call x1, Pallas kernels, per_device(): pl.pallas_call(kernel, out_shape=jax.ShapeDtypeStruct((1024, LMAX), F32),...  91.6 us
    unnamed x8, local copies, waits for them, and re-layouts  9.25 us

profile of v1, /device:TPU:6, one launch (start us, length us, event | category | flops | bytes accessed | tf_op | source)
XLA Modules:
  0.0 100.8 jit_solution(11068487886525609864)
XLA Ops:
  0.0 0.0 copy-start
  0.0 3.2 %copy.13.drift_hbm = f32[64,6,768]{2,1,0:T(8,128)} copy(f32[64,6,768]{2,0,1:T(8,128)} %param.13) | data formatting | bytes 2359296 | tf_op args[1]
  3.2 0.0 copy-done
  3.2 0.0 copy-start.1
  3.2 1.9 %copy.14.induce_hbm = f32[64,6,768]{2,1,0:T(8,128)} copy(f32[64,6,768]{2,0,1:T(8,128)S(1)} %copy-done) | data formatting | bytes 2359296 | tf_op args[2]
  5.1 0.0 copy-done.1
  5.1 1.9 %copy.15.couple_hbm = f32[64,6,768]{2,1,0:T(8,128)} copy(f32[64,6,768]{2,0,1:T(8,128)S(1)} %copy-done.1) | data formatting | bytes 2359296 | tf_op args[3]
  7.0 91.6 %shard_map.118 = f32[1024,256]{1,0:T(8,128)} custom-call(f32[1024,256]{1,0:T(8,128)} %bitcast.3, f32[64,6,768]{2,1,0:T(8,128)} %copy.13.drift_hbm, f32[64,6,768]{2,1,0:T(8,128)} %copy.14.induce_hbm, f32[64,6,768]{2,1,0:T(8,128)} %copy.15.couple_hbm, f32[4,2,336,128]{3,2,1,0:T(8,128)} %constant.16.clone.tri_hbm, f32[64,16,128]{2,1,0:T(8,128)} %constant.17.clone.start_hbm, ...), custom_call_target="tpu_custom_call" | custom-call | tf_op jit(solution)/shard_map/pallas_call | solution.py:447
  98.5 2.3 %copy.17 = f32[2,2,4,64,256]{4,3,2,1,0:T(8,128)} copy(f32[2,2,4,64,256]{4,3,2,1,0:T(8,128)} %bitcast.2) | data formatting | bytes 2097152
Async XLA Ops:
  0.0 3.2 %copy-start = (f32[64,6,768]{2,0,1:T(8,128)S(1)}, f32[64,6,768]{2,0,1:T(8,128)}, u32[]{:S(2)}) copy-start(f32[64,6,768]{2,0,1:T(8,128)} %param.14) | copy-start | bytes 3538948
  3.2 1.9 %copy-start.1 = (f32[64,6,768]{2,0,1:T(8,128)S(1)}, f32[64,6,768]{2,0,1:T(8,128)}, u32[]{:S(2)}) copy-start(f32[64,6,768]{2,0,1:T(8,128)} %param.15) | copy-start | bytes 3538948

commit v2 on v1

--- a/solution.py
+++ b/solution.py
@@ -173,7 +173,7 @@
     out_ref,
     adj, rel, tri, start, weight, tb, rise_ref, damp_ref, tth, ttl, rbh, rbl,
     ends, xs, xr, cs, yr, drift, induce, couple, mp, md, wh, wl, ah, al, acc,
-    in_sem, ends_send, ends_recv, xs_sem, xr_sem, cs_sem, yr_sem,
+    in_sem, out_sem, ends_send, ends_recv, xs_sem, xr_sem, cs_sem, yr_sem,
 ):
     rho = lax.axis_index("rad")
     me = lax.axis_index("ang")
@@ -347,7 +347,7 @@
                 at = (2 * part + field) * 64
                 rbh[order, at : at + 64, :] = high
                 rbl[order, at : at + 64, :] = low
-                acc[order, at : at + 64, :] = value
+                acc[rows, :] = value
 
     def send_part(part, source, target, send_sem, recv_sem):
         def send(step, unused):
@@ -390,9 +390,9 @@
         for block in range(6):
             cols = slice(128 * block, 128 * block + 128)
             scale = weight[t : t + 1, :]
-            pair = jnp.concatenate([couple[:, t, cols], induce[:, t, cols]], axis=0)
+            pair = jnp.concatenate([couple[t, :, cols], induce[t, :, cols]], axis=0)
             mp[t, cols, :] = pair.T * scale
-            turn = drift[:, t, cols]
+            turn = drift[t, :, cols]
             md[t, cols, :] = jnp.concatenate([turn, turn], axis=0).T * (-scale)
 
     for part in range(3):
@@ -415,6 +415,7 @@
         cs[second] = acc_c[:, 128:]
         send_part(part, cs, yr, cs_sem, yr_sem)
 
+    stores = []
     for part in range(3):
         wait_part(part, yr, yr_sem)
         rows = slice(128 * part, 128 * part + 128)
@@ -424,19 +425,27 @@
                 pair = [yr[2 * part + t, pl.ds(2 * order + trig, 64, stride=8), :] for t in range(2)]
                 sides.append(jnp.concatenate(pair, axis=0).T)
             value = split(jnp.concatenate(sides, axis=0))
-            acc[order] = acc[order] + product(value, (tth[order, rows, :], ttl[order, rows, :]), NN)
-
-    for order in range(4):
-        for trig in range(2):
-            for field in range(2):
-                at = ((2 * field + trig) * 4 + order) * 64
-                here = (2 * trig + field) * 64
-                out_ref[at : at + 64, :] = acc[order, here : here + 64, :]
+            value = product(value, (tth[order, rows, :], ttl[order, rows, :]), NN)
+            for trig in range(2):
+                for field in range(2):
+                    at = ((2 * field + trig) * 4 + order) * 64
+                    here = (2 * trig + field) * 64
+                    acc[at : at + 64, :] = acc[at : at + 64, :] + value[here : here + 64, :]
+                    if part == 2:
+                        result_rows = pl.ds(at, 64)
+                        stores.append(
+                            pltpu.make_async_copy(
+                                acc.at[result_rows], out_ref.at[result_rows], out_sem.at[len(stores)]
+                            )
+                        )
+                        stores[-1].start()
 
     pltpu.make_async_copy(block_ends, block_ends, ends_send).wait()
     for part in range(3):
         wait_part(part, xs, xs_sem)
         wait_part(part, cs, cs_sem)
+    for store in stores:
+        store.wait()
 
 
 def per_device(adjoint_in, drift, induce, couple):
@@ -448,7 +457,7 @@
         kernel,
         out_shape=jax.ShapeDtypeStruct((1024, LMAX), F32),
         in_specs=[anywhere] * 7 + [vmem] + [anywhere] * 4,
-        out_specs=vmem,
+        out_specs=anywhere,
         scratch_shapes=[
             pltpu.VMEM((2, 1024, 128), F32),
             pltpu.VMEM((2, 1024, 128), F32),
@@ -467,17 +476,18 @@
             pltpu.VMEM((6, 512, 128), F32),
             pltpu.VMEM((6, 512, 128), F32),
             pltpu.VMEM((6, 512, 128), F32),
-            pltpu.VMEM((SHELLS, 6, NLON), F32),
-            pltpu.VMEM((SHELLS, 6, NLON), F32),
-            pltpu.VMEM((SHELLS, 6, NLON), F32),
+            pltpu.VMEM((6, SHELLS, NLON), F32),
+            pltpu.VMEM((6, SHELLS, NLON), F32),
+            pltpu.VMEM((6, SHELLS, NLON), F32),
             pltpu.VMEM((6, NLON, 128), F32),
             pltpu.VMEM((6, NLON, 128), F32),
             pltpu.VMEM((3, 256, 512), BF16),
             pltpu.VMEM((3, 256, 512), BF16),
             pltpu.VMEM((3, 512, 512), BF16),
             pltpu.VMEM((3, 512, 512), BF16),
-            pltpu.VMEM((4, 256, LMAX), F32),
+            pltpu.VMEM((1024, LMAX), F32),
             pltpu.SemaphoreType.DMA((12,)),
+            pltpu.SemaphoreType.DMA((16,)),
             pltpu.SemaphoreType.DMA,
             pltpu.SemaphoreType.DMA,
             pltpu.SemaphoreType.DMA((3,)),
@@ -489,7 +499,8 @@
             collective_id=0, has_side_effects=True, vmem_limit_bytes=56 * 1024 * 1024
         ),
     )(
-        adjoint_in.reshape(1024, LMAX), drift, induce, couple,
+        adjoint_in.reshape(1024, LMAX),
+        drift.transpose(1, 0, 2), induce.transpose(1, 0, 2), couple.transpose(1, 0, 2),
         jnp.asarray(radial_constants()), jnp.asarray(start), jnp.asarray(weight_constants()),
         jnp.asarray(angle), jnp.asarray(wh), jnp.asarray(wl), jnp.asarray(ah), jnp.asarray(al),
     )

time: 102 us -> 94.6 us (0.927)
  local copies, waits for them, and re-layouts: 9.25 us -> 2.29 us
    unnamed x8 -> x1, local copies, waits for them, and re-layouts: 9.25 us -> 2.29 us
where the time goes in v2:
time: 94.6 us; the launch traced here: 93.3 us
  Pallas kernels  91 us (96%)
  local copies, waits for them, and re-layouts  2.29 us (2%)
    pallas_call x1, Pallas kernels, per_device(): pl.pallas_call(kernel, out_shape=jax.ShapeDtypeStruct((1024, LMAX), F32),...  91 us
    unnamed x1, local copies, waits for them, and re-layouts  2.29 us

profile of v2, /device:TPU:6, one launch (start us, length us, event | category | flops | bytes accessed | tf_op | source)
XLA Modules:
  0.0 93.3 jit_solution(10610194404543175520)
XLA Ops:
  0.0 91.0 %shard_map.118 = f32[1024,256]{1,0:T(8,128)} custom-call(f32[1024,256]{1,0:T(8,128)} %bitcast.9, f32[6,64,768]{2,1,0:T(8,128)} %bitcast.6, f32[6,64,768]{2,1,0:T(8,128)} %bitcast.7, f32[6,64,768]{2,1,0:T(8,128)} %bitcast.8, f32[4,2,336,128]{3,2,1,0:T(8,128)} %constant.16.clone.tri_hbm, f32[64,16,128]{2,1,0:T(8,128)} %constant.17.clone.start_hbm, ...), custom_call_target="tpu_custom_call" | custom-call | tf_op jit(solution)/shard_map/pallas_call | solution.py:456
  91.0 2.3 %copy.14 = f32[2,2,4,64,256]{4,3,2,1,0:T(8,128)} copy(f32[2,2,4,64,256]{4,3,2,1,0:T(8,128)} %bitcast.5) | data formatting | bytes 2097152

commit v3 on v2

--- a/solution.py
+++ b/solution.py
@@ -216,6 +216,62 @@
         pl.semaphore_signal(barrier, inc=1, device_id=(rad_peer(step), me), device_id_type=MESH)
     lax.fori_loop(1, ANG, greet, 0)
 
+    for load in loads[:3]:
+        load.wait()
+    row_id = lax.broadcasted_iota(jnp.int32, (16, 128), 0)
+    row_order = 4 * me + lax.rem(row_id, 4)
+    sine_zero = jnp.logical_and(row_order == 0, lax.rem(row_id // 4, 2) == 1)
+    lanes = lax.broadcasted_iota(jnp.int32, (16, 128), 1)
+    keeps = [
+        jnp.logical_and(lanes + 128 * half >= row_order, jnp.logical_not(sine_zero))
+        for half in range(2)
+    ]
+
+    def tri_row(row, half):
+        return tri[half, pl.ds(row, 1), :]
+
+    def sweep(row, carry):
+        result = []
+        for half in range(2):
+            right = adj[half, pl.ds(row, 16, stride=64), :]
+            right = jnp.where(keeps[half], right, 0.0) * tri_row(row, half)
+            value = right + tri_row(SHELLS + row, half) * carry[half]
+            rel[half, pl.ds(row, 16, stride=64), :] = value
+            result.append(value)
+        return tuple(result)
+
+    zero = jnp.zeros((16, 128), F32)
+    blank = jnp.where(keeps[0], 0.0, zero)
+    lax.fori_loop(0, SHELLS, sweep, (blank, blank), unroll=8)
+
+    def unsweep(step, carry):
+        row = SHELLS - 1 - step
+        result = []
+        for half in range(2):
+            value = rel[half, pl.ds(row, 16, stride=64), :]
+            value = value + tri_row(2 * SHELLS + row, half) * carry[half]
+            rel[half, pl.ds(row, 16, stride=64), :] = value
+            result.append(value)
+        return tuple(result)
+
+    lax.fori_loop(0, SHELLS, unsweep, (blank, blank), unroll=8)
+    for half in range(2):
+        for end, row in ((0, 0), (1, SHELLS - 1)):
+            ends[rho, pl.ds(16 * end, 16), 128 * half : 128 * half + 128] = rel[
+                half, pl.ds(row, 16, stride=64), :
+            ]
+
+    pl.semaphore_wait(barrier, ANG - 1 + RAD - 1)
+    for step in range(1, RAD):
+        pltpu.make_async_remote_copy(
+            src_ref=ends.at[rho],
+            dst_ref=ends.at[rho],
+            send_sem=ends_send,
+            recv_sem=ends_recv,
+            device_id=(rad_peer(step), me),
+            device_id_type=MESH,
+        ).start()
+
     lane_order = 4 * me + lax.broadcasted_iota(jnp.int32, (32, 128), 1) // 32
     order_f = lane_order.astype(F32)
 
@@ -232,62 +288,6 @@
         return unused
 
     lax.fori_loop(0, 8, factors, 0)
-
-    for load in loads[:3]:
-        load.wait()
-    row_id = lax.broadcasted_iota(jnp.int32, (16, 128), 0)
-    row_order = 4 * me + lax.rem(row_id, 4)
-    sine_zero = jnp.logical_and(row_order == 0, lax.rem(row_id // 4, 2) == 1)
-    lanes = lax.broadcasted_iota(jnp.int32, (16, 128), 1)
-    keeps = [
-        jnp.logical_and(lanes + 128 * half >= row_order, jnp.logical_not(sine_zero))
-        for half in range(2)
-    ]
-
-    def tri_row(row, half):
-        return tri[half, pl.ds(row, 1), :]
-
-    def sweep(row, carry):
-        result = []
-        for half in range(2):
-            right = adj[half, pl.ds(row, 16, stride=64), :]
-            right = jnp.where(keeps[half], right, 0.0) * tri_row(row, half)
-            value = right + tri_row(SHELLS + row, half) * carry[half]
-            rel[half, pl.ds(row, 16, stride=64), :] = value
-            result.append(value)
-        return tuple(result)
-
-    zero = jnp.zeros((16, 128), F32)
-    blank = jnp.where(keeps[0], 0.0, zero)
-    lax.fori_loop(0, SHELLS, sweep, (blank, blank), unroll=4)
-
-    def unsweep(step, carry):
-        row = SHELLS - 1 - step
-        result = []
-        for half in range(2):
-            value = rel[half, pl.ds(row, 16, stride=64), :]
-            value = value + tri_row(2 * SHELLS + row, half) * carry[half]
-            rel[half, pl.ds(row, 16, stride=64), :] = value
-            result.append(value)
-        return tuple(result)
-
-    lax.fori_loop(0, SHELLS, unsweep, (blank, blank), unroll=4)
-    for half in range(2):
-        for end, row in ((0, 0), (1, SHELLS - 1)):
-            ends[rho, pl.ds(16 * end, 16), 128 * half : 128 * half + 128] = rel[
-                half, pl.ds(row, 16, stride=64), :
-            ]
-
-    pl.semaphore_wait(barrier, ANG - 1 + RAD - 1)
-    for step in range(1, RAD):
-        pltpu.make_async_remote_copy(
-            src_ref=ends.at[rho],
-            dst_ref=ends.at[rho],
-            send_sem=ends_send,
-            recv_sem=ends_recv,
-            device_id=(rad_peer(step), me),
-            device_id_type=MESH,
-        ).start()
 
     loads[3].wait()
     cosine = angle_ref[...]

time: 94.6 us -> 94.9 us (level)
  no operation moved by 1% of the time
where the time goes in v3:
time: 94.9 us; the launch traced here: 93.2 us
  Pallas kernels  90.9 us (96%)
  local copies, waits for them, and re-layouts  2.29 us (2%)
    pallas_call x1, Pallas kernels, per_device(): pl.pallas_call(kernel, out_shape=jax.ShapeDtypeStruct((1024, LMAX), F32),...  90.9 us
    unnamed x1, local copies, waits for them, and re-layouts  2.29 us

profile of v3, /device:TPU:6, one launch (start us, length us, event | category | flops | bytes accessed | tf_op | source)
XLA Modules:
  0.0 93.2 jit_solution(5528935465356948554)
XLA Ops:
  0.0 90.9 %shard_map.118 = f32[1024,256]{1,0:T(8,128)} custom-call(f32[1024,256]{1,0:T(8,128)} %bitcast.9, f32[6,64,768]{2,1,0:T(8,128)} %bitcast.6, f32[6,64,768]{2,1,0:T(8,128)} %bitcast.7, f32[6,64,768]{2,1,0:T(8,128)} %bitcast.8, f32[4,2,336,128]{3,2,1,0:T(8,128)} %constant.16.clone.tri_hbm, f32[64,16,128]{2,1,0:T(8,128)} %constant.17.clone.start_hbm, ...), custom_call_target="tpu_custom_call" | custom-call | tf_op jit(solution)/shard_map/pallas_call | solution.py:456
  91.0 2.3 %copy.14 = f32[2,2,4,64,256]{4,3,2,1,0:T(8,128)} copy(f32[2,2,4,64,256]{4,3,2,1,0:T(8,128)} %bitcast.5) | data formatting | bytes 2097152
